TPU v7x, 256 devices: a whole 4x4x8 slice. The times are simulated.
256 devices in a mesh: gx: 8 (over x, y_lo), gy: 32 (over y_hi, z, core).
Axes of the slice: x: 4, y: 4 (y_hi: 2, y_lo: 2; y = y_hi * 2 + y_lo), z: 8, core: 2. Of those that a mesh axis runs over, the one named last changes fastest.
Arguments:
- state_field: bfloat16 [20, 64, 256, 256], P(None, 'gx', 'gy'), may hold values from -6 to 6
- conv_weight: bfloat16 [3, 20, 180], replicated, may hold values from -0.25 to 0.25
- spectral_weight: float32 [32, 32, 2, 20, 20, 16], P('gx', 'gy'), may hold values from -1 to 1
- channel_bias: float32 [20], replicated, may hold values from -3 to 3
Outputs:
- layer_out: bfloat16 [20, 64, 256, 256], P(None, 'gx', 'gy')
All inputs are finite; a program needn't handle non-finite values.
Results may differ from a plain program's by a relative error of at most 0.0032.
Values may be sent and summed in bfloat16 or wider, within the bound.
A program may use at most 128 MiB of HBM per device.

v0:
```python
import functools
import math

import jax
import jax.numpy as jnp
import ml_dtypes
import numpy as np
from jax import lax
from jax.experimental import pallas as pl
from jax.experimental.pallas import tpu as pltpu
from jax.sharding import PartitionSpec as P

MESH = pl.DeviceIdType.MESH
F32 = jnp.float32
BF16 = jnp.bfloat16
C = 20
NZ = 256
NX = 64
NY = 256
MX = 32
MY = 32
MZ = 16
GX = 8
GY = 32
LX = 8
LY = 8
ROWS = C * LY
GROUPS = 2 * C
PEERS = GX + GY - 2 + 4


def split(table):
    high = table.astype(np.float32).astype(ml_dtypes.bfloat16)
    low = (table - high.astype(np.float64)).astype(np.float32).astype(ml_dtypes.bfloat16)
    return np.stack([high, low])


def z_forward_table():
    z, k = np.arange(NZ)[:, None], np.arange(MZ)[None, :]
    angle = 2.0 * np.pi * (z * k % NZ) / NZ
    cos, sin = np.cos(angle), np.sin(angle)
    table = np.zeros((4, NZ, 2, 4, 2, MZ))
    for low in range(4):
        table[low, :, 0, low, 0] = cos
        table[low, :, 0, low, 1] = -sin
        table[low, :, 1, low, 0] = -sin
        table[low, :, 1, low, 1] = -cos
    return table.reshape(4 * NZ, 256).astype(np.float32).astype(ml_dtypes.bfloat16)


def z_inverse_table():
    k, z = np.arange(MZ)[:, None], np.arange(NZ)[None, :]
    angle = 2.0 * np.pi * (z * k % NZ) / NZ
    weight = np.where(k == 0, 1.0, 2.0) / math.sqrt(float(NX) * NY * NZ * 2.0 * MX * MY * MZ)
    cos, sin = np.cos(angle) * weight, np.sin(angle) * weight
    table = np.zeros((2, 4, 2, MZ, 4, NZ))
    for low in range(4):
        table[0, low, 0, :, low] = cos
        table[0, low, 1, :, low] = -sin
        table[1, low, 0, :, low] = -sin
        table[1, low, 1, :, low] = -cos
    return split(table.reshape(256, 4 * NZ))


def x_tables():
    kx = np.arange(MX)
    freq = np.where(kx < MX // 2, kx, kx - MX)
    angle = 2.0 * np.pi * (freq[None, :] * np.arange(LX)[:, None] % NX) / NX
    cos, sin = np.cos(angle), np.sin(angle)
    forward = np.zeros((LX, 2, MZ, MX, 2, MZ))
    inverse = np.zeros((MX, 2, MZ, LX, 2, MZ))
    for z in range(MZ):
        forward[:, 0, z, :, 0, z] = cos
        forward[:, 1, z, :, 0, z] = sin
        forward[:, 1, z, :, 1, z] = cos
        forward[:, 0, z, :, 1, z] = -sin
        inverse[:, 0, z, :, 0, z] = cos.T
        inverse[:, 1, z, :, 0, z] = -sin.T
        inverse[:, 1, z, :, 1, z] = cos.T
        inverse[:, 0, z, :, 1, z] = sin.T
    return split(forward.reshape(256, 1024)), split(inverse.reshape(1024, 256))


def spread_table():
    table = np.zeros((9 * C, 3, 3, 256), np.float32)
    for dz in range(3):
        for dy in range(3):
            base = (dy * 3 + dz) * C
            for c in range(C):
                table[base + c, dz, dy, c * LY : (c + 1) * LY] = 1.0
                table[base + c, dz, dy, ROWS + c] = 1.0
                table[base + c, dz, dy, ROWS + 32 + c] = 1.0
    return table.reshape(9 * C, 9 * 256).astype(ml_dtypes.bfloat16)


def edge_table():
    table = np.zeros((64, ROWS), np.float32)
    for c in range(C):
        table[c, c * LY + LY - 1] = 1.0
        table[32 + c, c * LY] = 1.0
    return table.astype(ml_dtypes.bfloat16)


def two_terms(value):
    high = value.astype(BF16)
    return high, (value - high.astype(F32)).astype(BF16)


def dot(a, b):
    return jnp.dot(a, b, preferred_element_type=F32)


def iota(shape, dim):
    return lax.broadcasted_iota(jnp.int32, shape, dim)


def turned(value, low):
    width = value.shape[1]
    return jnp.where(low, pltpu.roll(value, width - MZ, 1), pltpu.roll(value, MZ, 1))


def kernel(
    state, conv_w, bias, z_fwd, edge, x_fwd_hbm, x_inv_hbm, z_inv_hbm, spread_hbm, mix_hbm,
    out,
    x_fwd, x_inv, z_inv, spread, mix,
    cells, edges, band, conv, y_send, y_recv, x_send, x_recv, m_send, m_recv, joined, b_send, b_recv,
    y_inv, w_same, w_cross,
    load_sem, send_sem, recv_sem, halo_send, halo_recv,
):
    gx = lax.axis_index("gx")
    gy = lax.axis_index("gy")

    def along_x(step):
        return lax.rem(gx + step + GX, GX)

    def along_y(step):
        return lax.rem(gy + step + GY, GY)

    pairs = ((x_fwd_hbm, x_fwd), (x_inv_hbm, x_inv), (z_inv_hbm, z_inv), (spread_hbm, spread), (mix_hbm, mix))
    loads = [pltpu.make_async_copy(src, dst, load_sem.at[i]) for i, (src, dst) in enumerate(pairs)]
    for load in loads:
        load.start()

    barrier = pltpu.get_barrier_semaphore()

    @pl.loop(1, GY)
    def _(step):
        pl.semaphore_signal(barrier, inc=1, device_id={"gx": gx, "gy": along_y(step)}, device_id_type=MESH)

    @pl.loop(1, GX)
    def _(step):
        pl.semaphore_signal(barrier, inc=1, device_id={"gx": along_x(step), "gy": gy}, device_id_type=MESH)

    for dx in (-1, 1):
        for dy in (-1, 1):
            pl.semaphore_signal(
                barrier, inc=1, device_id={"gx": along_x(dx), "gy": along_y(dy)}, device_id_type=MESH
            )

    for x in range(LX):
        cells[x + 1, 0:ROWS] = state[:, x].astype(F32).reshape(ROWS, NZ).astype(BF16)
    wide = jnp.concatenate(
        [jnp.concatenate([cells[1 + low, 0:ROWS], cells[5 + low, 0:ROWS]], axis=0) for low in range(4)], axis=1
    )
    z_high, z_low = two_terms(dot(wide, z_fwd[...]))

    row, col = iota((256, 128), 0), iota((256, 128), 1)
    ky = (gy + row // 8) & (MY - 1)
    freq = jnp.where(ky < MY // 2, ky, ky - MY)
    angle = (freq * (gy * LY + (col & 7)) - 64 * (col // 64)) & (NY - 1)
    table = jnp.cos(angle.astype(F32) * (2.0 * math.pi / NY))
    t_high, t_low = two_terms(jnp.where((row & 7) == (col // 8 & 7), table, 0.0))

    def regroup(value):
        return jnp.concatenate(
            [
                jnp.concatenate([value[g * 64 : g * 64 + 64, 0:128], value[g * 64 : g * 64 + 64, 128:256]], axis=0)
                for g in range(5)
            ],
            axis=1,
        )

    z_high, z_low = regroup(z_high), regroup(z_low)
    y_part = dot(
        jnp.concatenate([t_high, t_high, t_low], axis=1), jnp.concatenate([z_high, z_low, z_high], axis=0)
    )
    for g in range(5):
        y_send[:, g * 8 : g * 8 + 8, :] = y_part[:, g * 128 : g * 128 + 128].reshape(GY, 8, 128).astype(BF16)

    pl.semaphore_wait(barrier, PEERS)

    @pl.loop(1, GY)
    def _(step):
        pltpu.make_async_remote_copy(
            src_ref=y_send.at[step],
            dst_ref=y_recv.at[step],
            send_sem=send_sem.at[0],
            recv_sem=recv_sem.at[0],
            device_id={"gx": gx, "gy": along_y(step)},
            device_id_type=MESH,
        ).start()

    for x in range(LX):
        picked = dot(edge[...], cells[x + 1, 0:ROWS]).astype(BF16)
        edges[0, x] = picked[0:32]
        edges[1, x] = picked[32:64]
    left, right = pl.ds(ROWS, 32), pl.ds(ROWS + 32, 32)
    main = pl.ds(0, ROWS)
    inner = pl.ds(1, LX)
    plan = [
        (edges.at[0], cells.at[inner, left], 0, 1),
        (edges.at[1], cells.at[inner, right], 0, -1),
        (cells.at[LX, main], cells.at[0, main], 1, 0),
        (cells.at[1, main], cells.at[LX + 1, main], -1, 0),
        (edges.at[0, LX - 1], cells.at[0, left], 1, 1),
        (edges.at[1, LX - 1], cells.at[0, right], 1, -1),
        (edges.at[0, 0], cells.at[LX + 1, left], -1, 1),
        (edges.at[1, 0], cells.at[LX + 1, right], -1, -1),
    ]
    halos = [
        pltpu.make_async_remote_copy(
            src_ref=src,
            dst_ref=dst,
            send_sem=halo_send.at[i],
            recv_sem=halo_recv.at[i],
            device_id={"gx": along_x(dx), "gy": along_y(dy)},
            device_id_type=MESH,
        )
        for i, (src, dst, dx, dy) in enumerate(plan)
    ]
    for halo in halos:
        halo.start()

    for x in range(LX + 2):
        cells[x, ROWS + 64 : 256] = jnp.zeros((32, NZ), BF16)
    loads[3].wait()
    repeat = (iota((ROWS, C), 0) // LY == iota((ROWS, C), 1)).astype(F32).astype(BF16)
    y_row, cell = iota((ROWS, 256), 0) & 7, iota((ROWS, 256), 1)
    y_col = jnp.where(cell < ROWS, cell & 7, jnp.where(cell < ROWS + 32, -1, jnp.where(cell < ROWS + 64, 8, 100)))
    masks = [y_col == y_row + dy - 1 for dy in range(3)]
    for dx in range(3):
        lines = dot(repeat, conv_w[dx]).astype(BF16)
        for dz in range(3):
            total = jnp.zeros((ROWS, 256), F32)
            for dy in range(3):
                at = (dz * 3 + dy) * 256
                total = jnp.where(masks[dy], dot(lines, spread[:, at : at + 256]), total)
            band[dz * ROWS : (dz + 1) * ROWS, dx * 256 : (dx + 1) * 256] = total.astype(BF16)
    pick = iota((ROWS, C), 0) // LY == iota((ROWS, C), 1)
    bias_rows = jnp.sum(jnp.where(pick, bias[...], 0.0), axis=1, keepdims=True)

    loads[4].wait()
    low20 = (iota((C, 128), 1) & 31) < MZ

    @pl.loop(0, C)
    def _(i):
        lines = jnp.transpose(mix[:, :, i].reshape(128, C))
        w_same[i] = jnp.where(low20, lines, pltpu.roll(lines, MZ, 1))
        w_cross[i] = jnp.where(low20, -pltpu.roll(lines, 128 - MZ, 1), lines)

    row, col = iota((128, 256), 0), iota((128, 256), 1)
    ky = (gy + GY - col // 8) & (MY - 1)
    freq = jnp.where(ky < MY // 2, ky, ky - MY)
    angle = (freq * (gy * LY + (row & 7)) - 64 * (row // 64)) & (NY - 1)
    table = jnp.cos(angle.astype(F32) * (2.0 * math.pi / NY))
    t_high, t_low = two_terms(jnp.where((row // 8 & 7) == (col & 7), table, 0.0))
    y_inv[0] = t_high
    y_inv[1] = t_low

    kx = iota((8, 1024), 1) // 32
    turn = (kx * gx) & 7
    low1 = (iota((8, 1024), 1) & 31) < MZ
    phase_cos = jnp.cos(turn.astype(F32) * (2.0 * math.pi / 8))[0:1]
    phase_sin = jnp.cos(((turn + 6) & 7).astype(F32) * (2.0 * math.pi / 8))
    phase_sin = jnp.where(low1, phase_sin, -phase_sin)[0:1]
    low32 = (iota((32, 1024), 1) & 31) < MZ

    def y_copies():
        return pltpu.make_async_remote_copy(
            src_ref=y_send.at[pl.ds(1, GY - 1)],
            dst_ref=y_recv.at[pl.ds(1, GY - 1)],
            send_sem=send_sem.at[0],
            recv_sem=recv_sem.at[0],
            device_id={"gx": gx, "gy": along_y(1)},
            device_id_type=MESH,
        )

    def x_copies(ref, which):
        return pltpu.make_async_remote_copy(
            src_ref=ref.at[pl.ds(1, GX - 1)],
            dst_ref=ref.at[pl.ds(1, GX - 1)],
            send_sem=send_sem.at[which],
            recv_sem=recv_sem.at[which],
            device_id={"gx": along_x(1), "gy": gy},
            device_id_type=MESH,
        )

    y_copies().wait_recv()
    total = y_send[0].astype(F32)
    for step in range(1, GY):
        total = total + y_recv[step].astype(F32)
    pad = jnp.zeros((12, 256), F32)
    total = jnp.concatenate([jnp.concatenate([total[0:C], total[C:GROUPS]], axis=1), pad], axis=0)
    loads[0].wait()
    s_high, s_low = two_terms(total)
    both = dot(jnp.concatenate([s_high, s_low], axis=0), x_fwd[0])
    x_part = both[0:32] + both[32:64] + dot(s_high, x_fwd[1])
    x_part = x_part * phase_cos + turned(x_part, low32) * phase_sin
    for g in range(GX):
        x_send[g] = x_part[0:24, g * 128 : g * 128 + 128]

    @pl.loop(1, GX)
    def _(step):
        to = along_x(step)
        pltpu.make_async_remote_copy(
            src_ref=x_send.at[to],
            dst_ref=x_recv.at[step],
            send_sem=send_sem.at[1],
            recv_sem=recv_sem.at[1],
            device_id={"gx": to, "gy": gy},
            device_id_type=MESH,
        ).start()

    for halo in halos:
        halo.wait_recv()

    def convolve(x):
        window = cells[pl.ds(x, 3)].reshape(768, NZ)
        taps = dot(band[...], window)
        conv[x] = (
            pltpu.roll(taps[0:ROWS], 1, 1)
            + taps[ROWS : 2 * ROWS]
            + pltpu.roll(taps[2 * ROWS : 3 * ROWS], NZ - 1, 1)
            + bias_rows
        )

    @pl.loop(0, 4)
    def _(x):
        convolve(x)

    x_copies(x_recv, 1).wait_recv()
    modes = x_send[gx]
    for step in range(1, GX):
        modes = modes + x_recv[step]
    crossed = turned(modes, (iota((24, 128), 1) & 31) < MZ)
    mixed = jnp.zeros((C, 128), F32)
    for i in range(C):
        mixed = mixed + w_same[i] * modes[i : i + 1] + w_cross[i] * crossed[i : i + 1]
    m_send[...] = jnp.concatenate([mixed, jnp.zeros((4, 128), F32)], axis=0)

    @pl.loop(1, GX)
    def _(step):
        pltpu.make_async_remote_copy(
            src_ref=m_send,
            dst_ref=m_recv.at[step],
            send_sem=send_sem.at[2],
            recv_sem=recv_sem.at[2],
            device_id={"gx": along_x(step), "gy": gy},
            device_id_type=MESH,
        ).start()

    @pl.loop(4, LX)
    def _(x):
        convolve(x)

    x_copies(m_recv, 2).wait_recv()
    joined[24:32] = jnp.zeros((8, 1024), F32)
    joined[0:24, pl.ds(pl.multiple_of(gx * 128, 128), 128)] = m_send[...]
    for step in range(1, GX):
        joined[0:24, pl.ds(pl.multiple_of(along_x(-step) * 128, 128), 128)] = m_recv[step]
    total = joined[...]
    total = total * phase_cos - turned(total, low32) * phase_sin
    loads[1].wait()
    s_high, s_low = two_terms(total)
    both = dot(jnp.concatenate([s_high, s_low], axis=0), x_inv[0])
    x_back = both[0:32] + both[32:64] + dot(s_high, x_inv[1])
    x_back = jnp.concatenate([x_back[0:C, 0:128], x_back[0:C, 128:256]], axis=0).astype(BF16)
    b_send[...] = x_back
    b_recv[0] = x_back

    @pl.loop(1, GY)
    def _(step):
        pltpu.make_async_remote_copy(
            src_ref=b_send,
            dst_ref=b_recv.at[step],
            send_sem=send_sem.at[3],
            recv_sem=recv_sem.at[3],
            device_id={"gx": gx, "gy": along_y(step)},
            device_id_type=MESH,
        ).start()

    all_b = pltpu.make_async_remote_copy(
        src_ref=b_recv.at[pl.ds(1, GY - 1)],
        dst_ref=b_recv.at[pl.ds(1, GY - 1)],
        send_sem=send_sem.at[3],
        recv_sem=recv_sem.at[3],
        device_id={"gx": gx, "gy": along_y(1)},
        device_id_type=MESH,
    )
    loads[2].wait()
    all_b.wait_recv()
    parts = [b_recv[:, g * 8 : g * 8 + 8, :].astype(F32).reshape(256, 128).astype(BF16) for g in range(5)]
    parts = jnp.concatenate(parts, axis=1)
    back = dot(y_inv[0], parts) + dot(y_inv[1], parts)
    back = jnp.concatenate(
        [
            jnp.concatenate([back[0:64, g * 128 : g * 128 + 128], back[64:128, g * 128 : g * 128 + 128]], axis=1)
            for g in range(5)
        ],
        axis=0,
    )
    u_high, u_low = two_terms(back)
    for low in range(4):
        at = low * NZ
        spectral = (
            dot(u_high, z_inv[0, :, at : at + NZ])
            + dot(u_low, z_inv[0, :, at : at + NZ])
            + dot(u_high, z_inv[1, :, at : at + NZ])
        )
        for high in range(2):
            x = high * 4 + low
            value = conv[x] + spectral[high * ROWS : (high + 1) * ROWS]
            value = jax.nn.gelu(value)
            out[:, x] = value.reshape(C, LY, NZ).astype(BF16)

    y_copies().wait_send()
    for halo in halos:
        halo.wait_send()
    x_copies(x_send, 1).wait_send()
    x_copies(m_recv, 2).wait_send()
    all_b.wait_send()


def on_device(state_field, conv_weight, spectral_weight, channel_bias):
    mix = jnp.transpose(spectral_weight[:, 0], (0, 1, 2, 4, 3))
    x_fwd, x_inv = x_tables()
    vmem, hbm = pl.BlockSpec(memory_space=pltpu.VMEM), pl.BlockSpec(memory_space=pl.ANY)
    return pl.pallas_call(
        kernel,
        out_shape=jax.ShapeDtypeStruct((C, LX, LY, NZ), BF16),
        in_specs=[vmem] * 5 + [hbm] * 5,
        out_specs=vmem,
        scratch_shapes=[
            pltpu.VMEM((2, 256, 1024), BF16),
            pltpu.VMEM((2, 1024, 256), BF16),
            pltpu.VMEM((2, 256, 1024), BF16),
            pltpu.VMEM((9 * C, 9 * 256), BF16),
            pltpu.VMEM((4, 2, C, MZ, C), F32),
            pltpu.VMEM((LX + 2, 256, NZ), BF16),
            pltpu.VMEM((2, LX, 32, NZ), BF16),
            pltpu.VMEM((3 * ROWS, 768), BF16),
            pltpu.VMEM((LX, ROWS, NZ), F32),
            pltpu.VMEM((GY, GROUPS, 128), BF16),
            pltpu.VMEM((GY, GROUPS, 128), BF16),
            pltpu.VMEM((GX, 24, 128), F32),
            pltpu.VMEM((GX, 24, 128), F32),
            pltpu.VMEM((24, 128), F32),
            pltpu.VMEM((GX, 24, 128), F32),
            pltpu.VMEM((32, 1024), F32),
            pltpu.VMEM((GROUPS, 128), BF16),
            pltpu.VMEM((GY, GROUPS, 128), BF16),
            pltpu.VMEM((2, 128, 256), BF16),
            pltpu.VMEM((C, C, 128), F32),
            pltpu.VMEM((C, C, 128), F32),
            pltpu.SemaphoreType.DMA((5,)),
            pltpu.SemaphoreType.DMA((4,)),
            pltpu.SemaphoreType.DMA((4,)),
            pltpu.SemaphoreType.DMA((8,)),
            pltpu.SemaphoreType.DMA((8,)),
        ],
        compiler_params=pltpu.CompilerParams(
            collective_id=0, has_side_effects=True, vmem_limit_bytes=48 * 1024 * 1024
        ),
        cost_estimate=pl.CostEstimate(flops=800_000_000, bytes_accessed=8_000_000, transcendentals=400_000),
    )(
        state_field,
        conv_weight,
        channel_bias.reshape(1, C),
        jnp.asarray(z_forward_table()),
        jnp.asarray(edge_table()),
        jnp.asarray(x_fwd),
        jnp.asarray(x_inv),
        jnp.asarray(z_inverse_table()),
        jnp.asarray(spread_table()),
        mix,
    )


def solution(mesh):
    return jax.shard_map(
        on_device,
        mesh=mesh,
        in_specs=(P(None, "gx", "gy", None), P(), P("gx", "gy", None, None, None, None), P()),
        out_specs=P(None, "gx", "gy", None),
        check_vma=False,
    )
```

profile of v0, /device:TPU:1, one launch (start us, length us, event | category | flops | bytes accessed | tf_op | source)
XLA Modules:
  0.0 54.1 jit_solution(8469448827056305981)
XLA Ops:
  0.0 0.0 copy-start
  0.0 1.2 %copy-done = bf16[2,256,1024]{2,1,0:T(8,128)(2,1)S(1)} copy-done((bf16[2,256,1024]{2,1,0:T(8,128)(2,1)S(1)}, bf16[2,256,1024]{2,1,0:T(8,128)(2,1)}, u32[]{:S(2)}) %copy-start) | copy-done | bytes 1048600
  1.2 0.0 copy-start.1
  1.2 1.2 %copy-done.1 = bf16[2,1024,256]{2,1,0:T(8,128)(2,1)S(1)} copy-done((bf16[2,1024,256]{2,1,0:T(8,128)(2,1)S(1)}, bf16[2,1024,256]{2,1,0:T(8,128)(2,1)}, u32[]{:S(2)}) %copy-start.1) | copy-done | bytes 1048600
  2.5 0.0 copy-start.2
  2.5 1.2 %copy-done.2 = bf16[2,256,1024]{2,1,0:T(8,128)(2,1)S(1)} copy-done((bf16[2,256,1024]{2,1,0:T(8,128)(2,1)S(1)}, bf16[2,256,1024]{2,1,0:T(8,128)(2,1)}, u32[]{:S(2)}) %copy-start.2) | copy-done | bytes 1048600
  3.7 0.0 copy-start.3
  3.7 1.2 %copy-done.3 = bf16[180,2304]{1,0:T(8,128)(2,1)S(1)} copy-done((bf16[180,2304]{1,0:T(8,128)(2,1)S(1)}, bf16[180,2304]{1,0:T(8,128)(2,1)}, u32[]{:S(2)}) %copy-start.3) | copy-done | bytes 829464
  4.8 0.0 copy-start.4
  4.8 1.1 %copy-done.4 = bf16[20,8,8,256]{3,2,1,0:T(8,128)(2,1)S(1)} copy-done((bf16[20,8,8,256]{3,2,1,0:T(8,128)(2,1)S(1)}, bf16[20,8,8,256]{3,2,1,0:T(8,128)(2,1)}, u32[]{:S(2)}) %copy-start.4) | copy-done | bytes 655384
  5.9 0.0 copy-start.5
  5.9 1.0 %copy-done.5 = bf16[1024,256]{1,0:T(8,128)(2,1)S(1)} copy-done((bf16[1024,256]{1,0:T(8,128)(2,1)S(1)}, bf16[1024,256]{1,0:T(8,128)(2,1)}, u32[]{:S(2)}) %copy-start.5) | copy-done | bytes 524312
  7.0 0.0 copy-start.6
  7.0 0.8 %copy-done.6 = bf16[3,20,180]{2,1,0:T(8,128)(2,1)S(1)} copy-done((bf16[3,20,180]{2,1,0:T(8,128)(2,1)S(1)}, bf16[3,20,180]{2,1,0:T(8,128)(2,1)}, u32[]{:S(2)}) %copy-start.6) | copy-done | bytes 21624
  7.7 0.0 copy-start.7
  7.7 0.8 %copy-done.7 = bf16[64,160]{1,0:T(8,128)(2,1)S(1)} copy-done((bf16[64,160]{1,0:T(8,128)(2,1)S(1)}, bf16[64,160]{1,0:T(8,128)(2,1)}, u32[]{:S(2)}) %copy-start.7) | copy-done | bytes 20504
  8.5 0.0 copy-start.8
  8.5 0.7 %copy-done.8 = f32[20]{0:T(128)S(1)} copy-done((f32[20]{0:T(128)S(1)}, f32[20]{0:T(128)}, u32[]{:S(2)}) %copy-start.8) | copy-done | bytes 104
  9.1 44.1 %shard_map.100 = bf16[20,8,8,256]{3,2,1,0:T(8,128)(2,1)S(1)} custom-call(bf16[20,8,8,256]{3,2,1,0:T(8,128)(2,1)S(1)} %copy-done.4, bf16[3,20,180]{2,1,0:T(8,128)(2,1)S(1)} %copy-done.6, f32[1,20]{1,0:T(1,128)S(1)} %bitcast.4, bf16[1024,256]{1,0:T(8,128)(2,1)S(1)} %copy-done.5, bf16[64,160]{1,0:T(8,128)(2,1)S(1)} %copy-done.7, ...), custom_call_target="tpu_custom_call" | custom-call | flops 800000000 | bytes 8000000 | tf_op jit(solution)/shard_map/pallas_call | solution.py:438
  53.3 0.8 %copy.12 = bf16[20,8,8,256]{3,2,1,0:T(8,128)(2,1)} copy(bf16[20,8,8,256]{3,2,1,0:T(8,128)(2,1)S(1)} %shard_map.100) | data formatting | bytes 1310720
Async XLA Ops:
  0.0 1.2 %copy-start = (bf16[2,256,1024]{2,1,0:T(8,128)(2,1)S(1)}, bf16[2,256,1024]{2,1,0:T(8,128)(2,1)}, u32[]{:S(2)}) copy-start(bf16[2,256,1024]{2,1,0:T(8,128)(2,1)} %constant.16.clone.z_inv_hbm) | copy-start | bytes 3145732
  1.2 1.2 %copy-start.1 = (bf16[2,1024,256]{2,1,0:T(8,128)(2,1)S(1)}, bf16[2,1024,256]{2,1,0:T(8,128)(2,1)}, u32[]{:S(2)}) copy-start(bf16[2,1024,256]{2,1,0:T(8,128)(2,1)} %constant.15.clone.x_inv_hbm) | copy-start | bytes 3145732
  2.5 1.2 %copy-start.2 = (bf16[2,256,1024]{2,1,0:T(8,128)(2,1)S(1)}, bf16[2,256,1024]{2,1,0:T(8,128)(2,1)}, u32[]{:S(2)}) copy-start(bf16[2,256,1024]{2,1,0:T(8,128)(2,1)} %constant.14.clone.x_fwd_hbm) | copy-start | bytes 3145732
  3.7 1.2 %copy-start.3 = (bf16[180,2304]{1,0:T(8,128)(2,1)S(1)}, bf16[180,2304]{1,0:T(8,128)(2,1)}, u32[]{:S(2)}) copy-start(bf16[180,2304]{1,0:T(8,128)(2,1)} %constant.17.clone.spread_hbm) | copy-start | bytes 2488324
  4.8 1.1 %copy-start.4 = (bf16[20,8,8,256]{3,2,1,0:T(8,128)(2,1)S(1)}, bf16[20,8,8,256]{3,2,1,0:T(8,128)(2,1)}, u32[]{:S(2)}) copy-start(bf16[20,8,8,256]{3,2,1,0:T(8,128)(2,1)} %state.1) | copy-start | bytes 1966084
  5.9 1.0 %copy-start.5 = (bf16[1024,256]{1,0:T(8,128)(2,1)S(1)}, bf16[1024,256]{1,0:T(8,128)(2,1)}, u32[]{:S(2)}) copy-start(bf16[1024,256]{1,0:T(8,128)(2,1)} %constant.12.clone.z_fwd) | copy-start | bytes 1572868
  7.0 0.8 %copy-start.6 = (bf16[3,20,180]{2,1,0:T(8,128)(2,1)S(1)}, bf16[3,20,180]{2,1,0:T(8,128)(2,1)}, u32[]{:S(2)}) copy-start(bf16[3,20,180]{2,1,0:T(8,128)(2,1)} %conv_w.1) | copy-start | bytes 64804
  7.7 0.8 %copy-start.7 = (bf16[64,160]{1,0:T(8,128)(2,1)S(1)}, bf16[64,160]{1,0:T(8,128)(2,1)}, u32[]{:S(2)}) copy-start(bf16[64,160]{1,0:T(8,128)(2,1)} %constant.13.clone.edge) | copy-start | bytes 61444
  8.5 0.7 %copy-start.8 = (f32[20]{0:T(128)S(1)}, f32[20]{0:T(128)}, u32[]{:S(2)}) copy-start(f32[20]{0:T(128)} %param.13) | copy-start | bytes 244
where the time goes:
time: 54.6 us; the launch traced here: 54.1 us
  Pallas kernels  44.1 us (81%)
  local copies, waits for them, and re-layouts  9.97 us (18%)
    pallas_call x1, Pallas kernels, on_device(): pl.pallas_call(kernel, out_shape=jax.ShapeDtypeStruct((C, LX, LY, NZ), BF...  44.1 us
    unnamed x19, local copies, waits for them, and re-layouts  9.97 us

commit v1 on v0

--- a/solution.py
+++ b/solution.py
@@ -120,9 +120,9 @@
 
 
 def kernel(
-    state, conv_w, bias, z_fwd, edge, x_fwd_hbm, x_inv_hbm, z_inv_hbm, spread_hbm, mix_hbm,
+    state_hbm, z_fwd_hbm, edge_hbm, x_fwd_hbm, x_inv_hbm, z_inv_hbm, spread_hbm, mix_hbm, conv_w_hbm, bias_hbm,
     out,
-    x_fwd, x_inv, z_inv, spread, mix,
+    state, z_fwd, edge, x_fwd, x_inv, z_inv, spread, mix, conv_w, bias,
     cells, edges, band, conv, y_send, y_recv, x_send, x_recv, m_send, m_recv, joined, b_send, b_recv,
     y_inv, w_same, w_cross,
     load_sem, send_sem, recv_sem, halo_send, halo_recv,
@@ -136,8 +136,23 @@
     def along_y(step):
         return lax.rem(gy + step + GY, GY)
 
-    pairs = ((x_fwd_hbm, x_fwd), (x_inv_hbm, x_inv), (z_inv_hbm, z_inv), (spread_hbm, spread), (mix_hbm, mix))
-    loads = [pltpu.make_async_copy(src, dst, load_sem.at[i]) for i, (src, dst) in enumerate(pairs)]
+    loads = [
+        pltpu.make_async_copy(src, dst, load_sem.at[i])
+        for i, (src, dst) in enumerate(
+            (
+                (state_hbm, state),
+                (z_fwd_hbm, z_fwd),
+                (edge_hbm, edge),
+                (conv_w_hbm, conv_w),
+                (spread_hbm, spread),
+                (bias_hbm, bias),
+                (mix_hbm, mix),
+                (x_fwd_hbm, x_fwd),
+                (x_inv_hbm, x_inv),
+                (z_inv_hbm, z_inv),
+            )
+        )
+    ]
     for load in loads:
         load.start()
 
@@ -156,13 +171,6 @@
             pl.semaphore_signal(
                 barrier, inc=1, device_id={"gx": along_x(dx), "gy": along_y(dy)}, device_id_type=MESH
             )
-
-    for x in range(LX):
-        cells[x + 1, 0:ROWS] = state[:, x].astype(F32).reshape(ROWS, NZ).astype(BF16)
-    wide = jnp.concatenate(
-        [jnp.concatenate([cells[1 + low, 0:ROWS], cells[5 + low, 0:ROWS]], axis=0) for low in range(4)], axis=1
-    )
-    z_high, z_low = two_terms(dot(wide, z_fwd[...]))
 
     row, col = iota((256, 128), 0), iota((256, 128), 1)
     ky = (gy + row // 8) & (MY - 1)
@@ -170,6 +178,15 @@
     angle = (freq * (gy * LY + (col & 7)) - 64 * (col // 64)) & (NY - 1)
     table = jnp.cos(angle.astype(F32) * (2.0 * math.pi / NY))
     t_high, t_low = two_terms(jnp.where((row & 7) == (col // 8 & 7), table, 0.0))
+
+    loads[0].wait()
+    for x in range(LX):
+        cells[x + 1, 0:ROWS] = state[:, x].astype(F32).reshape(ROWS, NZ).astype(BF16)
+    wide = jnp.concatenate(
+        [jnp.concatenate([cells[1 + low, 0:ROWS], cells[5 + low, 0:ROWS]], axis=0) for low in range(4)], axis=1
+    )
+    loads[1].wait()
+    z_high, z_low = two_terms(dot(wide, z_fwd[...]))
 
     def regroup(value):
         return jnp.concatenate(
@@ -200,6 +217,7 @@
             device_id_type=MESH,
         ).start()
 
+    loads[2].wait()
     for x in range(LX):
         picked = dot(edge[...], cells[x + 1, 0:ROWS]).astype(BF16)
         edges[0, x] = picked[0:32]
@@ -234,6 +252,8 @@
     for x in range(LX + 2):
         cells[x, ROWS + 64 : 256] = jnp.zeros((32, NZ), BF16)
     loads[3].wait()
+    loads[4].wait()
+    loads[5].wait()
     repeat = (iota((ROWS, C), 0) // LY == iota((ROWS, C), 1)).astype(F32).astype(BF16)
     y_row, cell = iota((ROWS, 256), 0) & 7, iota((ROWS, 256), 1)
     y_col = jnp.where(cell < ROWS, cell & 7, jnp.where(cell < ROWS + 32, -1, jnp.where(cell < ROWS + 64, 8, 100)))
@@ -249,7 +269,7 @@
     pick = iota((ROWS, C), 0) // LY == iota((ROWS, C), 1)
     bias_rows = jnp.sum(jnp.where(pick, bias[...], 0.0), axis=1, keepdims=True)
 
-    loads[4].wait()
+    loads[6].wait()
     low20 = (iota((C, 128), 1) & 31) < MZ
 
     @pl.loop(0, C)
@@ -301,7 +321,7 @@
         total = total + y_recv[step].astype(F32)
     pad = jnp.zeros((12, 256), F32)
     total = jnp.concatenate([jnp.concatenate([total[0:C], total[C:GROUPS]], axis=1), pad], axis=0)
-    loads[0].wait()
+    loads[7].wait()
     s_high, s_low = two_terms(total)
     both = dot(jnp.concatenate([s_high, s_low], axis=0), x_fwd[0])
     x_part = both[0:32] + both[32:64] + dot(s_high, x_fwd[1])
@@ -370,7 +390,7 @@
         joined[0:24, pl.ds(pl.multiple_of(along_x(-step) * 128, 128), 128)] = m_recv[step]
     total = joined[...]
     total = total * phase_cos - turned(total, low32) * phase_sin
-    loads[1].wait()
+    loads[8].wait()
     s_high, s_low = two_terms(total)
     both = dot(jnp.concatenate([s_high, s_low], axis=0), x_inv[0])
     x_back = both[0:32] + both[32:64] + dot(s_high, x_inv[1])
@@ -397,7 +417,7 @@
         device_id={"gx": gx, "gy": along_y(1)},
         device_id_type=MESH,
     )
-    loads[2].wait()
+    loads[9].wait()
     all_b.wait_recv()
     parts = [b_recv[:, g * 8 : g * 8 + 8, :].astype(F32).reshape(256, 128).astype(BF16) for g in range(5)]
     parts = jnp.concatenate(parts, axis=1)
@@ -434,18 +454,23 @@
 def on_device(state_field, conv_weight, spectral_weight, channel_bias):
     mix = jnp.transpose(spectral_weight[:, 0], (0, 1, 2, 4, 3))
     x_fwd, x_inv = x_tables()
-    vmem, hbm = pl.BlockSpec(memory_space=pltpu.VMEM), pl.BlockSpec(memory_space=pl.ANY)
+    vmem, hbm = pl.BlockSpec(memory_space=pltpu.VMEM), pl.BlockSpec(memory_space=pltpu.HBM)
     return pl.pallas_call(
         kernel,
         out_shape=jax.ShapeDtypeStruct((C, LX, LY, NZ), BF16),
-        in_specs=[vmem] * 5 + [hbm] * 5,
+        in_specs=[hbm] * 10,
         out_specs=vmem,
         scratch_shapes=[
+            pltpu.VMEM((C, LX, LY, NZ), BF16),
+            pltpu.VMEM((4 * NZ, 256), BF16),
+            pltpu.VMEM((64, ROWS), BF16),
             pltpu.VMEM((2, 256, 1024), BF16),
             pltpu.VMEM((2, 1024, 256), BF16),
             pltpu.VMEM((2, 256, 1024), BF16),
             pltpu.VMEM((9 * C, 9 * 256), BF16),
             pltpu.VMEM((4, 2, C, MZ, C), F32),
+            pltpu.VMEM((3, C, 9 * C), BF16),
+            pltpu.VMEM((1, C), F32),
             pltpu.VMEM((LX + 2, 256, NZ), BF16),
             pltpu.VMEM((2, LX, 32, NZ), BF16),
             pltpu.VMEM((3 * ROWS, 768), BF16),
@@ -462,20 +487,18 @@
             pltpu.VMEM((2, 128, 256), BF16),
             pltpu.VMEM((C, C, 128), F32),
             pltpu.VMEM((C, C, 128), F32),
-            pltpu.SemaphoreType.DMA((5,)),
+            pltpu.SemaphoreType.DMA((10,)),
             pltpu.SemaphoreType.DMA((4,)),
             pltpu.SemaphoreType.DMA((4,)),
             pltpu.SemaphoreType.DMA((8,)),
             pltpu.SemaphoreType.DMA((8,)),
         ],
         compiler_params=pltpu.CompilerParams(
-            collective_id=0, has_side_effects=True, vmem_limit_bytes=48 * 1024 * 1024
+            collective_id=0, has_side_effects=True, vmem_limit_bytes=60 * 1024 * 1024
         ),
         cost_estimate=pl.CostEstimate(flops=800_000_000, bytes_accessed=8_000_000, transcendentals=400_000),
     )(
         state_field,
-        conv_weight,
-        channel_bias.reshape(1, C),
         jnp.asarray(z_forward_table()),
         jnp.asarray(edge_table()),
         jnp.asarray(x_fwd),
@@ -483,6 +506,8 @@
         jnp.asarray(z_inverse_table()),
         jnp.asarray(spread_table()),
         mix,
+        conv_weight,
+        channel_bias.reshape(1, C),
     )
 
 

time: 54.6 us -> 46.8 us (0.86)
  local copies, waits for them, and re-layouts: 9.97 us -> 1.98 us
  Pallas kernels: 44.1 us -> 44.7 us
    unnamed x19 -> x1, local copies, waits for them, and re-layouts: 9.97 us -> 1.98 us
    pallas_call x1, Pallas kernels: 44.1 us -> 44.7 us  [on_device(): pl.pallas_call(kernel, out_shape=jax.ShapeDtypeStruct((C, LX, LY, NZ), BF...]
where the time goes in v1:
time: 46.8 us; the launch traced here: 46.7 us
  Pallas kernels  44.7 us (96%)
  local copies, waits for them, and re-layouts  1.98 us (4%)
    pallas_call x1, Pallas kernels, on_device(): pl.pallas_call(kernel, out_shape=jax.ShapeDtypeStruct((C, LX, LY, NZ), BF...  44.7 us
    unnamed x1, local copies, waits for them, and re-layouts  1.98 us

profile of v1, /device:TPU:1, one launch (start us, length us, event | category | flops | bytes accessed | tf_op | source)
XLA Modules:
  0.0 46.7 jit_solution(1042992138522175983)
XLA Ops:
  0.0 44.7 %shard_map.100 = bf16[20,8,8,256]{3,2,1,0:T(8,128)(2,1)} custom-call(bf16[20,8,8,256]{3,2,1,0:T(8,128)(2,1)} %state_hbm.1, bf16[1024,256]{1,0:T(8,128)(2,1)} %constant.12.clone.z_fwd_hbm, bf16[64,160]{1,0:T(8,128)(2,1)} %constant.13.clone.edge_hbm, bf16[2,256,1024]{2,1,0:T(8,128)(2,1)} %constant.14.clone.x_fwd_hbm, ...), custom_call_target="tpu_custom_call" | custom-call | flops 800000000 | bytes 8000000 | tf_op jit(solution)/shard_map/pallas_call | solution.py:458
  44.7 2.0 %copy.12 = bf16[20,8,8,256]{3,2,1,0:T(8,128)(2,1)} copy(bf16[20,8,8,256]{3,2,1,0:T(8,128)(2,1)} %shard_map.100) | data formatting | bytes 1310720

commit v2 on v1

v2 whole, which is shorter than its diff:
```python
import functools
import math

import jax
import jax.numpy as jnp
import ml_dtypes
import numpy as np
from jax import lax
from jax.experimental import pallas as pl
from jax.experimental.pallas import tpu as pltpu
from jax.sharding import PartitionSpec as P

MESH = pl.DeviceIdType.MESH
F32 = jnp.float32
BF16 = jnp.bfloat16
C = 20
NZ = 256
NX = 64
NY = 256
MX = 32
MY = 32
MZ = 16
GX = 8
GY = 32
LX = 8
LY = 8
ROWS = C * LY
GROUPS = 2 * C
SAME = GY // 2
PEERS = (SAME - 1) + 2 + (GX - 1) + 4
X_FWD = 4 * NZ
EARLY = 5
FAR_Y = (4, 12, 3, 5, 11, 13, 2, 6, 10, 14, 8, 1, 7, 9, 15)
FAR_X = (4, 3, 5, 2, 6, 1, 7)
X_INV = X_FWD + 2048
Z_INV = X_INV + 2048


def split(table):
    high = table.astype(np.float32).astype(ml_dtypes.bfloat16)
    low = (table - high.astype(np.float64)).astype(np.float32).astype(ml_dtypes.bfloat16)
    return np.stack([high, low])


def z_forward_table():
    z, k = np.arange(NZ)[:, None], np.arange(MZ)[None, :]
    angle = 2.0 * np.pi * (z * k % NZ) / NZ
    cos, sin = np.cos(angle), np.sin(angle)
    table = np.zeros((4, NZ, 2, 4, 2, MZ))
    for low in range(4):
        table[low, :, 0, low, 0] = cos
        table[low, :, 0, low, 1] = -sin
        table[low, :, 1, low, 0] = -sin
        table[low, :, 1, low, 1] = -cos
    return table.reshape(4 * NZ, 256).astype(np.float32).astype(ml_dtypes.bfloat16)


def z_inverse_table():
    k, z = np.arange(MZ)[:, None], np.arange(NZ)[None, :]
    angle = 2.0 * np.pi * (z * k % NZ) / NZ
    weight = np.where(k == 0, 1.0, 2.0) / math.sqrt(float(NX) * NY * NZ * 2.0 * MX * MY * MZ)
    cos, sin = np.cos(angle) * weight, np.sin(angle) * weight
    table = np.zeros((2, 4, 2, MZ, 4, NZ))
    for low in range(4):
        table[0, low, 0, :, low] = cos
        table[0, low, 1, :, low] = -sin
        table[1, low, 0, :, low] = -sin
        table[1, low, 1, :, low] = -cos
    return split(table.reshape(256, 4 * NZ))


def x_tables():
    kx = np.arange(MX)
    freq = np.where(kx < MX // 2, kx, kx - MX)
    angle = 2.0 * np.pi * (freq[None, :] * np.arange(LX)[:, None] % NX) / NX
    cos, sin = np.cos(angle), np.sin(angle)
    forward = np.zeros((LX, 2, MZ, MX, 2, MZ))
    inverse = np.zeros((MX, 2, MZ, LX, 2, MZ))
    for z in range(MZ):
        forward[:, 0, z, :, 0, z] = cos
        forward[:, 1, z, :, 0, z] = sin
        forward[:, 1, z, :, 1, z] = cos
        forward[:, 0, z, :, 1, z] = -sin
        inverse[:, 0, z, :, 0, z] = cos.T
        inverse[:, 1, z, :, 0, z] = -sin.T
        inverse[:, 1, z, :, 1, z] = cos.T
        inverse[:, 0, z, :, 1, z] = sin.T
    return split(forward.reshape(256, 1024)), split(inverse.reshape(1024, 256))


def spread_table():
    table = np.zeros((9 * C, 3, 3, 256), np.float32)
    for dz in range(3):
        for dy in range(3):
            base = (dy * 3 + dz) * C
            for c in range(C):
                table[base + c, dz, dy, c * LY : (c + 1) * LY] = 1.0
                table[base + c, dz, dy, ROWS + c] = 1.0
                table[base + c, dz, dy, ROWS + 32 + c] = 1.0
    return table.reshape(9 * C, 9 * 256).astype(ml_dtypes.bfloat16)


def tables():
    x_fwd, x_inv = x_tables()
    blocks = [z_forward_table()]
    blocks += [x_fwd[term, :, n * 256 : n * 256 + 256] for term in range(2) for n in range(4)]
    blocks += [x_inv[0], x_inv[1]]
    z_inv = z_inverse_table()
    blocks += [z_inv[term, :, n * 256 : n * 256 + 256] for term in range(2) for n in range(4)]
    return np.concatenate(blocks, axis=0)


def two_terms(value):
    high = value.astype(BF16)
    return high, (value - high.astype(F32)).astype(BF16)


def dot(a, b):
    return jnp.dot(a, b, preferred_element_type=F32)


def iota(shape, dim):
    return lax.broadcasted_iota(jnp.int32, shape, dim)


def turned(value, low):
    width = value.shape[1]
    return jnp.where(low, pltpu.roll(value, width - MZ, 1), pltpu.roll(value, MZ, 1))


def kernel(
    state_hbm, tables_hbm, small_hbm, spread_hbm, mix_hbm,
    out,
    state, table, small, spread, mix,
    cells, edges, band, conv, z_send, z_recv, y_send, y_recv, x_send, x_recv, m_send, m_recv, joined, b_send, b_recv,
    y_inv, w_same, w_cross,
    load_sem, send_sem, recv_sem, b_send_sem, b_recv_sem, halo_send, halo_recv,
):
    gx = lax.axis_index("gx")
    gy = lax.axis_index("gy")

    def along_x(step):
        return lax.rem(gx + step + GX, GX)

    def along_y(step):
        return lax.rem(gy + step + GY, GY)

    core = lax.rem(gy, 2)
    other = gy + 1 - 2 * core

    barrier = pltpu.get_barrier_semaphore()
    peers = [(0, 2 * step) for step in FAR_Y] + [(dx, dy) for dy in (-1, 1) for dx in (-1, 0, 1)]
    peers += [(step, 0) for step in FAR_X]
    for dx, dy in peers:
        pl.semaphore_signal(
            barrier, inc=1, device_id={"gx": along_x(dx), "gy": along_y(dy)}, device_id_type=MESH
        )

    def rows_of_table(first, count):
        return tables_hbm.at[pl.ds(first, count)], table.at[pl.ds(first, count)]

    loads = [
        pltpu.make_async_copy(src, dst, load_sem.at[i])
        for i, (src, dst) in enumerate(
            (
                (state_hbm, state),
                rows_of_table(0, X_FWD),
                (small_hbm, small),
                (spread_hbm, spread),
                (mix_hbm, mix),
                rows_of_table(X_FWD, 2048),
                rows_of_table(X_INV, 2048),
                rows_of_table(Z_INV, 2048),
            )
        )
    ]
    for load in loads:
        load.start()

    row, col = iota((128, 256), 0), iota((128, 256), 1)
    ky = (gy + row // 8 * 2) & (MY - 1)
    freq = jnp.where(ky < MY // 2, ky, ky - MY)
    place = jnp.where(col < 128, gy, other) * LY + (col & 7)
    angle = (freq * place - (col & 64)) & (NY - 1)
    turns = jnp.cos(angle.astype(F32) * (2.0 * math.pi / NY))
    t_high, t_low = two_terms(jnp.where((row & 7) == (col // 8 & 7), turns, 0.0))

    loads[0].wait()
    for x in range(LX):
        cells[x + 1, 0:ROWS] = state[:, x].astype(F32).reshape(ROWS, NZ).astype(BF16)
    wide = jnp.concatenate(
        [jnp.concatenate([cells[1 + low, 0:ROWS], cells[5 + low, 0:ROWS]], axis=0) for low in range(4)], axis=1
    )
    loads[1].wait()
    spectrum = dot(wide, table[0:X_FWD])

    def regroup(value, first):
        return jnp.concatenate([value[g * 64 : g * 64 + 64, first : first + 128] for g in range(5)], axis=1)

    plain, crossed = regroup(spectrum, 0), regroup(spectrum, 128)
    z_send[...] = plain
    pl.semaphore_wait(barrier, PEERS)
    exchange = pltpu.make_async_remote_copy(
        src_ref=z_send,
        dst_ref=z_recv,
        send_sem=send_sem.at[4],
        recv_sem=recv_sem.at[4],
        device_id={"gx": gx, "gy": other},
        device_id_type=MESH,
    )
    exchange.start()

    left, right = pl.ds(ROWS, 32), pl.ds(ROWS + 32, 32)
    main = pl.ds(0, ROWS)
    inner = pl.ds(1, LX)
    plan = [
        (edges.at[0], cells.at[inner, left], 0, 1),
        (edges.at[1], cells.at[inner, right], 0, -1),
        (cells.at[LX, main], cells.at[0, main], 1, 0),
        (cells.at[1, main], cells.at[LX + 1, main], -1, 0),
        (edges.at[0, LX - 1], cells.at[0, left], 1, 1),
        (edges.at[1, LX - 1], cells.at[0, right], 1, -1),
        (edges.at[0, 0], cells.at[LX + 1, left], -1, 1),
        (edges.at[1, 0], cells.at[LX + 1, right], -1, -1),
    ]
    halos = [
        pltpu.make_async_remote_copy(
            src_ref=src,
            dst_ref=dst,
            send_sem=halo_send.at[i],
            recv_sem=halo_recv.at[i],
            device_id={"gx": along_x(dx), "gy": along_y(dy)},
            device_id_type=MESH,
        )
        for i, (src, dst, dx, dy) in enumerate(plan)
    ]
    for halo in halos[2:4]:
        halo.start()

    def y_product(plain, crossed, first):
        high, low = two_terms(jnp.concatenate([plain, crossed], axis=0))
        left_high, left_low = t_high[:, first : first + 128], t_low[:, first : first + 128]
        return dot(
            jnp.concatenate([left_high, left_high, left_low], axis=1), jnp.concatenate([high, low, high], axis=0)
        )

    y_part = y_product(plain, crossed, 0)
    exchange.wait_recv()
    plain = z_recv[...]
    low64 = (iota((64, 640), 1) & 31) < MZ
    crossed = jnp.where(low64, pltpu.roll(plain, 640 - MZ, 1), -pltpu.roll(plain, MZ, 1))
    y_part = y_part + y_product(plain, crossed, 128)
    for g in range(5):
        y_send[:, g * 8 : g * 8 + 8, :] = y_part[:, g * 128 : g * 128 + 128].reshape(SAME, 8, 128).astype(BF16)

    for step in FAR_Y:
        pltpu.make_async_remote_copy(
            src_ref=y_send.at[step],
            dst_ref=y_recv.at[step],
            send_sem=send_sem.at[0],
            recv_sem=recv_sem.at[0],
            device_id={"gx": gx, "gy": along_y(2 * step)},
            device_id_type=MESH,
        ).start()

    row, col = iota((64, ROWS), 0), iota((64, ROWS), 1)
    last = jnp.where(row < C, row * LY + LY - 1, -1)
    first = jnp.where(row - 32 < C, (row - 32) * LY, -1)
    edge = (col == jnp.where(row < 32, last, first)).astype(F32).astype(BF16)
    for x in range(LX):
        picked = dot(edge, cells[x + 1, 0:ROWS]).astype(BF16)
        edges[0, x] = picked[0:32]
        edges[1, x] = picked[32:64]
    for halo in halos[:2] + halos[4:]:
        halo.start()

    for x in range(LX + 2):
        cells[x, ROWS + 64 : 256] = jnp.zeros((32, NZ), BF16)
    loads[2].wait()
    loads[3].wait()
    repeat = (iota((ROWS, C), 0) // LY == iota((ROWS, C), 1)).astype(F32).astype(BF16)
    y_row, cell = iota((ROWS, 256), 0) & 7, iota((ROWS, 256), 1)
    y_col = jnp.where(cell < ROWS, cell & 7, jnp.where(cell < ROWS + 32, -1, jnp.where(cell < ROWS + 64, 8, 100)))
    masks = [y_col == y_row + dy - 1 for dy in range(3)]
    for dx in range(3):
        lines = dot(repeat, small[dx, 0:C].astype(BF16)).astype(BF16)[:, 0 : 9 * C]
        for dz in range(3):
            total = jnp.zeros((ROWS, 256), F32)
            for dy in range(3):
                at = (dz * 3 + dy) * 256
                total = jnp.where(masks[dy], dot(lines, spread[:, at : at + 256]), total)
            band[dz * ROWS : (dz + 1) * ROWS, dx * 256 : (dx + 1) * 256] = total.astype(BF16)
    pick = iota((ROWS, C), 0) // LY == iota((ROWS, C), 1)
    bias_rows = jnp.sum(jnp.where(pick, small[0, 24:25, 0:C], 0.0), axis=1, keepdims=True)

    loads[4].wait()
    low20 = (iota((C, 128), 1) & 31) < MZ

    @pl.loop(0, C)
    def _(i):
        lines = jnp.transpose(mix[:, :, i].reshape(128, C))
        w_same[i] = jnp.where(low20, lines, pltpu.roll(lines, MZ, 1))
        w_cross[i] = jnp.where(low20, -pltpu.roll(lines, 128 - MZ, 1), lines)

    row, col = iota((128, 256), 0), iota((128, 256), 1)
    ky = (jnp.where(col < 128, gy, other) + GY - 2 * (col // 8 & (SAME - 1))) & (MY - 1)
    freq = jnp.where(ky < MY // 2, ky, ky - MY)
    angle = (freq * (gy * LY + (row & 7)) - 64 * (row // 64)) & (NY - 1)
    turns = jnp.cos(angle.astype(F32) * (2.0 * math.pi / NY))
    t_high, t_low = two_terms(jnp.where((row // 8 & 7) == (col & 7), turns, 0.0))
    y_inv[0] = t_high
    y_inv[1] = t_low

    kx = iota((8, 1024), 1) // 32
    turn = (kx * gx) & 7
    low1 = (iota((8, 1024), 1) & 31) < MZ
    phase_cos = jnp.cos(turn.astype(F32) * (2.0 * math.pi / 8))[0:1]
    phase_sin = jnp.cos(((turn + 6) & 7).astype(F32) * (2.0 * math.pi / 8))
    phase_sin = jnp.where(low1, phase_sin, -phase_sin)[0:1]
    low32 = (iota((32, 1024), 1) & 31) < MZ

    def y_copies():
        return pltpu.make_async_remote_copy(
            src_ref=y_send.at[pl.ds(1, SAME - 1)],
            dst_ref=y_recv.at[pl.ds(1, SAME - 1)],
            send_sem=send_sem.at[0],
            recv_sem=recv_sem.at[0],
            device_id={"gx": gx, "gy": along_y(2)},
            device_id_type=MESH,
        )

    def x_copies(ref, which):
        return pltpu.make_async_remote_copy(
            src_ref=ref.at[pl.ds(1, GX - 1)],
            dst_ref=ref.at[pl.ds(1, GX - 1)],
            send_sem=send_sem.at[which],
            recv_sem=recv_sem.at[which],
            device_id={"gx": along_x(1), "gy": gy},
            device_id_type=MESH,
        )

    y_copies().wait_recv()
    total = y_send[0].astype(F32)
    for step in range(1, SAME):
        total = total + y_recv[step].astype(F32)
    pad = jnp.zeros((12, 256), F32)
    total = jnp.concatenate([jnp.concatenate([total[0:C], total[C:GROUPS]], axis=1), pad], axis=0)
    loads[5].wait()
    s_high, s_low = two_terms(total)
    s_both = jnp.concatenate([s_high, s_low], axis=0)

    def x_block(term, n):
        at = X_FWD + (term * 4 + n) * 256
        return table[at : at + 256]

    both = jnp.concatenate([dot(s_both, x_block(0, n)) for n in range(4)], axis=1)
    x_part = both[0:32] + both[32:64] + jnp.concatenate([dot(s_high, x_block(1, n)) for n in range(4)], axis=1)
    x_part = x_part * phase_cos + turned(x_part, low32) * phase_sin
    for g in range(GX):
        x_send[g] = x_part[0:24, g * 128 : g * 128 + 128]

    for step in FAR_X:
        to = along_x(step)
        pltpu.make_async_remote_copy(
            src_ref=x_send.at[to],
            dst_ref=x_recv.at[step],
            send_sem=send_sem.at[1],
            recv_sem=recv_sem.at[1],
            device_id={"gx": to, "gy": gy},
            device_id_type=MESH,
        ).start()

    x_copies(x_recv, 1).wait_recv()
    modes = x_send[gx]
    for step in range(1, GX):
        modes = modes + x_recv[step]
    crossed = turned(modes, (iota((24, 128), 1) & 31) < MZ)
    mixed = jnp.zeros((C, 128), F32)
    for i in range(C):
        mixed = mixed + w_same[i] * modes[i : i + 1] + w_cross[i] * crossed[i : i + 1]
    m_send[...] = jnp.concatenate([mixed, jnp.zeros((4, 128), F32)], axis=0)

    for step in FAR_X:
        pltpu.make_async_remote_copy(
            src_ref=m_send,
            dst_ref=m_recv.at[step],
            send_sem=send_sem.at[2],
            recv_sem=recv_sem.at[2],
            device_id={"gx": along_x(step), "gy": gy},
            device_id_type=MESH,
        ).start()

    for halo in halos:
        halo.wait_recv()

    def convolve(x):
        window = cells[pl.ds(x, 3)].reshape(768, NZ)
        taps = dot(band[...], window)
        conv[x] = (
            pltpu.roll(taps[0:ROWS], 1, 1)
            + taps[ROWS : 2 * ROWS]
            + pltpu.roll(taps[2 * ROWS : 3 * ROWS], NZ - 1, 1)
            + bias_rows
        )

    @pl.loop(0, EARLY)
    def _(x):
        convolve(x)

    x_copies(m_recv, 2).wait_recv()
    joined[24:32] = jnp.zeros((8, 1024), F32)
    joined[0:24, pl.ds(pl.multiple_of(gx * 128, 128), 128)] = m_send[...]
    for step in range(1, GX):
        joined[0:24, pl.ds(pl.multiple_of(along_x(-step) * 128, 128), 128)] = m_recv[step]
    total = joined[...]
    total = total * phase_cos - turned(total, low32) * phase_sin
    loads[6].wait()
    s_high, s_low = two_terms(total)
    both = dot(jnp.concatenate([s_high, s_low], axis=0), table[X_INV : X_INV + 1024])
    x_back = both[0:32] + both[32:64] + dot(s_high, table[X_INV + 1024 : X_INV + 2048])
    x_back = jnp.concatenate([x_back[0:C, 0:128], x_back[0:C, 128:256]], axis=0).astype(BF16)
    b_send[0] = x_back
    b_recv[0] = x_back

    def to_other(src, first, count, which):
        return pltpu.make_async_remote_copy(
            src_ref=src,
            dst_ref=b_recv.at[pl.ds(first, count)],
            send_sem=send_sem.at[which],
            recv_sem=recv_sem.at[which],
            device_id={"gx": gx, "gy": other},
            device_id_type=MESH,
        )

    def b_copy(step):
        return pltpu.make_async_remote_copy(
            src_ref=b_send.at[0],
            dst_ref=b_recv.at[step],
            send_sem=b_send_sem.at[step],
            recv_sem=b_recv_sem.at[step],
            device_id={"gx": gx, "gy": along_y(2 * step)},
            device_id_type=MESH,
        )

    for step in FAR_Y:
        b_copy(step).start()

    handed = [to_other(b_send, SAME, 1, 3)]
    handed[0].start()

    @pl.loop(EARLY, LX)
    def _(x):
        convolve(x)

    for step in reversed(FAR_Y):
        b_copy(step).wait_recv()
        handed.append(to_other(b_recv.at[pl.ds(step, 1)], SAME + step, 1, 4 + step))
        handed[-1].start()

    loads[7].wait()
    for copy in handed:
        copy.wait_recv()
    parts = [b_recv[:, g * 8 : g * 8 + 8, :].astype(F32).reshape(256, 128).astype(BF16) for g in range(5)]
    parts = jnp.concatenate(parts, axis=1)
    back = dot(y_inv[0], parts) + dot(y_inv[1], parts)
    back = jnp.concatenate(
        [
            jnp.concatenate([back[0:64, g * 128 : g * 128 + 128], back[64:128, g * 128 : g * 128 + 128]], axis=1)
            for g in range(5)
        ],
        axis=0,
    )
    u_high, u_low = two_terms(back)
    for low in range(4):
        at = Z_INV + low * 256
        rough, fine = table[at : at + 256], table[at + 1024 : at + 1280]
        spectral = dot(u_high, rough) + dot(u_low, rough) + dot(u_high, fine)
        for high in range(2):
            x = high * 4 + low
            value = conv[x] + spectral[high * ROWS : (high + 1) * ROWS]
            value = jax.nn.gelu(value)
            out[:, x] = value.reshape(C, LY, NZ).astype(BF16)

    y_copies().wait_send()
    for halo in halos:
        halo.wait_send()
    x_copies(x_send, 1).wait_send()
    x_copies(m_recv, 2).wait_send()
    exchange.wait_send()
    for step in FAR_Y:
        b_copy(step).wait_send()
    for copy in handed:
        copy.wait_send()


def on_device(state_field, conv_weight, spectral_weight, channel_bias):
    mix = jnp.transpose(spectral_weight[:, 0], (0, 1, 2, 4, 3))
    small = jnp.pad(conv_weight.astype(F32), ((0, 0), (0, 32 - C), (0, 256 - 9 * C)))
    small = small + jnp.pad(channel_bias.reshape(1, 1, C), ((0, 2), (24, 7), (0, 256 - C)))
    vmem, hbm = pl.BlockSpec(memory_space=pltpu.VMEM), pl.BlockSpec(memory_space=pltpu.HBM)
    return pl.pallas_call(
        kernel,
        out_shape=jax.ShapeDtypeStruct((C, LX, LY, NZ), BF16),
        in_specs=[hbm] * 5,
        out_specs=vmem,
        scratch_shapes=[
            pltpu.VMEM((C, LX, LY, NZ), BF16),
            pltpu.VMEM((Z_INV + 2048, 256), BF16),
            pltpu.VMEM((3, 32, 256), F32),
            pltpu.VMEM((9 * C, 9 * 256), BF16),
            pltpu.VMEM((4, 2, C, MZ, C), F32),
            pltpu.VMEM((LX + 2, 256, NZ), BF16),
            pltpu.VMEM((2, LX, 32, NZ), BF16),
            pltpu.VMEM((3 * ROWS, 768), BF16),
            pltpu.VMEM((LX, ROWS, NZ), F32),
            pltpu.VMEM((64, 640), F32),
            pltpu.VMEM((64, 640), F32),
            pltpu.VMEM((SAME, GROUPS, 128), BF16),
            pltpu.VMEM((SAME, GROUPS, 128), BF16),
            pltpu.VMEM((GX, 24, 128), F32),
            pltpu.VMEM((GX, 24, 128), F32),
            pltpu.VMEM((24, 128), F32),
            pltpu.VMEM((GX, 24, 128), F32),
            pltpu.VMEM((32, 1024), F32),
            pltpu.VMEM((1, GROUPS, 128), BF16),
            pltpu.VMEM((GY, GROUPS, 128), BF16),
            pltpu.VMEM((2, 128, 256), BF16),
            pltpu.VMEM((C, C, 128), F32),
            pltpu.VMEM((C, C, 128), F32),
            pltpu.SemaphoreType.DMA((8,)),
            pltpu.SemaphoreType.DMA((20,)),
            pltpu.SemaphoreType.DMA((20,)),
            pltpu.SemaphoreType.DMA((SAME,)),
            pltpu.SemaphoreType.DMA((SAME,)),
            pltpu.SemaphoreType.DMA((8,)),
            pltpu.SemaphoreType.DMA((8,)),
        ],
        compiler_params=pltpu.CompilerParams(
            collective_id=0, has_side_effects=True, vmem_limit_bytes=54000 * 1024
        ),
        cost_estimate=pl.CostEstimate(flops=800_000_000, bytes_accessed=8_000_000, transcendentals=400_000),
    )(
        state_field,
        jnp.asarray(tables()),
        small,
        jnp.asarray(spread_table()),
        mix,
    )


def solution(mesh):
    return jax.shard_map(
        on_device,
        mesh=mesh,
        in_specs=(P(None, "gx", "gy", None), P(), P("gx", "gy", None, None, None, None), P()),
        out_specs=P(None, "gx", "gy", None),
        check_vma=False,
    )
```

time: 46.8 us -> 41.1 us (0.88)
  Pallas kernels: 44.7 us -> 39.4 us
  local copies, waits for them, and re-layouts: 1.98 us -> 0.84 us
  other arithmetic: 0 us -> 0.79 us
    pallas_call x1, Pallas kernels: 44.7 us -> 39.4 us  [on_device(): pl.pallas_call(kernel, out_shape=jax.ShapeDtypeStruct((C, LX, LY, NZ), BF...]
    unnamed x1, local copies, waits for them, and re-layouts: 1.98 us -> 0.84 us
    add x0 -> x1, other arithmetic: none -> 0.79 us  [on_device(): small + jnp.pad(channel_bias.reshape(1, 1, C), ((0, 2), (24, 7), (0, 256...]
where the time goes in v2:
time: 41.1 us; the launch traced here: 41 us
  Pallas kernels  39.4 us (96%)
  local copies, waits for them, and re-layouts  0.84 us (2%)
  other arithmetic  0.79 us (2%)
    pallas_call x1, Pallas kernels, on_device(): pl.pallas_call(kernel, out_shape=jax.ShapeDtypeStruct((C, LX, LY, NZ), BF...  39.4 us
    unnamed x1, local copies, waits for them, and re-layouts  0.84 us

profile of v2, /device:TPU:1, one launch (start us, length us, event | category | flops | bytes accessed | tf_op | source)
XLA Modules:
  0.0 41.0 jit_solution(15750286040043001822)
XLA Ops:
  0.0 0.8 %pad_add_fusion.small_hbm = f32[3,32,256]{2,1,0:T(8,128)S(1)} fusion(f32[1,1,20]{2,1,0:T(1,128)} %bitcast.5, bf16[3,20,180]{2,1,0:T(8,128)(2,1)} %param.7), kind=kLoop, calls=%fused_computation | loop fusion | flops 49152 | bytes 119984 | tf_op jit(solution)/shard_map/add | solution.py:499
  0.8 39.4 %shard_map.64 = bf16[20,8,8,256]{3,2,1,0:T(8,128)(2,1)S(1)} custom-call(bf16[20,8,8,256]{3,2,1,0:T(8,128)(2,1)} %state_hbm.1, bf16[7168,256]{1,0:T(8,128)(2,1)} %constant.9.clone.tables_hbm, f32[3,32,256]{2,1,0:T(8,128)S(1)} %pad_add_fusion.small_hbm, bf16[180,2304]{1,0:T(8,128)(2,1)} %constant.10.clone.spread_hbm, f32[4,2,20,16,20]{4,3,2,1,0:T(8,128)} %bitcast.4), custom_call_target="tpu_custom_call" | custom-call | flops 800000000 | bytes 8000000 | tf_op jit(solution)/shard_map/pallas_call | solution.py:501
  40.2 0.8 %copy.8 = bf16[20,8,8,256]{3,2,1,0:T(8,128)(2,1)} copy(bf16[20,8,8,256]{3,2,1,0:T(8,128)(2,1)S(1)} %shard_map.64) | data formatting | bytes 1310720
